TPU v7x, 256 devices: a whole 4x4x8 slice. The times are simulated.
256 devices in a mesh: sx: 32 (over x, y, core), sy: 8 (over z).
Axes of the slice: x: 4, y: 4, z: 8, core: 2. Of those that a mesh axis runs over, the one named last changes fastest.
Arguments:
- start_block: float32 [64, 1048576], P(None, ('sx', 'sy'))
- blocks: float32 [7, 64, 1048576], P(None, None, ('sx', 'sy')), may hold values from -0.25 to 0.25
- neighbors: int32 [6, 16384], P(None, ('sx', 'sy')), may hold values from 0 to 95, as said below
- ghost_lists: int32 [32, 8, 4, 8], P('sx', 'sy'), may hold values from 0 to 63, as said below
Outputs:
- q_basis: float32 [192, 1048576], P(None, ('sx', 'sy'))
- r_factor: float32 [192, 192], replicated
Inputs may be any that keep to these rules, and one draw needn't show every extreme that they name: `neighbors`: values 0 to 63 name a local element; 64 + d * 8 + g names ghost slot g of direction d. Every ghost slot is named by some entry of every subdomain. `ghost_lists`: the 8 entries of one list are distinct.
All inputs are finite; a program needn't handle non-finite values.
Results may differ from a plain program's by a relative error of at most 0.00016.
Values sent between devices are 32-bit elements; how exact they have to be, the bound alone decides.
A program may use at most 192 MiB of HBM per device.

v0:
```python
import jax
import jax.numpy as jnp
from jax import lax
from jax.sharding import PartitionSpec as P


def from_behind(value, axis, steps):
    count = lax.axis_size(axis)
    pairs = [(source, (source + steps) % count) for source in range(count)]
    return lax.ppermute(value, axis, pairs)


def shards(start_block, blocks, neighbors, ghost_lists):
    count_rhs, rows = start_block.shape
    nodes = blocks.shape[1]
    elems = rows // nodes
    lists = ghost_lists[0, 0]
    ghosts = lists.shape[1]
    own_index = jnp.arange(elems, dtype=jnp.int32)[None, :]
    index = jnp.concatenate([own_index, neighbors], axis=0)
    tiles = blocks.reshape(7, nodes, elems, nodes)

    def apply_operator(vec):
        grid = vec.reshape(count_rhs, elems, nodes)
        sends = jnp.take(grid, lists, axis=1).reshape(count_rhs, 4, ghosts * nodes)
        from_x_low = from_behind(sends[:, 0], "sx", 1)
        from_x_high = from_behind(sends[:, 1], "sx", -1)
        from_y_low = from_behind(sends[:, 2], "sy", 1)
        from_y_high = from_behind(sends[:, 3], "sy", -1)
        arrived = [
            piece.reshape(count_rhs, ghosts, nodes)
            for piece in (from_x_low, from_x_high, from_y_low, from_y_high)
        ]
        extended = jnp.concatenate([grid] + arrived, axis=1)
        picked = jnp.take(extended, index, axis=1)
        result = jnp.einsum("zkec,kcer->zer", picked, tiles, precision=lax.Precision.HIGHEST)
        return result.reshape(count_rhs, rows)

    power_one = apply_operator(start_block)
    power_two = apply_operator(power_one)
    basis = jnp.concatenate([start_block, power_one, power_two], axis=0)
    gram = lax.psum(jnp.dot(basis, basis.T, precision=lax.Precision.HIGHEST), ("sx", "sy"))
    lower = jnp.linalg.cholesky(gram)
    orthonormal = jax.scipy.linalg.solve_triangular(lower, basis, lower=True)
    total_rows = rows * lax.axis_size("sx") * lax.axis_size("sy")
    scale = jnp.sqrt(jnp.float32(total_rows))
    return (orthonormal * scale, lower.T / scale)


def solution(mesh):
    return jax.shard_map(
        shards,
        mesh=mesh,
        in_specs=(
            P(None, ("sx", "sy")),
            P(None, None, ("sx", "sy")),
            P(None, ("sx", "sy")),
            P("sx", "sy", None, None),
        ),
        out_specs=(P(None, ("sx", "sy")), P()),
        check_vma=False,
    )
```

profile of v0, /device:TPU:1, one launch (start us, length us, event | category | flops | bytes accessed | tf_op | source)
XLA Modules:
  0.0 529.3 jit_solution(7927775227982481918)
XLA Ops:
  8.6 3.1 reshape.79
  11.7 4.1 fusion.38
  15.9 3.2 gather_fusion
  19.1 2.9 fusion.26
  30.4 3.9 collective-permute-start.3
  34.5 12.6 %reshape.85 = f32[7,64,64,64]{3,2,1,0:T(8,128)} reshape(f32[7,64,4096]{2,1,0:T(8,128)} %param.9) | data formatting | bytes 14680064 | tf_op jit(solution)/shard_map/reshape | solution.py:21
  50.5 6.3 %gather_fusion.1 = f32[448,64,64]{2,1,0:T(8,128)} fusion(f32[64,96,64]{2,0,1:T(8,128)S(1)} %copy_dynamic-update-slice_fusion.4, s32[1024]{0:T(1024)S(1)} %pad_clamp_fusion), kind=kCustom, calls=%fused_computation.1.clone | custom fusion | bytes 14681856 | tf_op jit(solution)/shard_map/jit(_take)/gather | solution.py:35
  56.8 14.9 %copy.57 = f32[7,64,64,64]{1,0,3,2:T(8,128)} copy(f32[7,64,64,64]{3,2,1,0:T(8,128)} %bitcast.82) | data formatting | bytes 14680064 | tf_op jit(solution)/shard_map/jit(_take)/gather | solution.py:35
  71.8 11.6 %select_bitcast_fusion = f32[64,7,64,64]{2,1,3,0:T(8,128)} fusion(f32[7,64,64,64]{1,0,3,2:T(8,128)} %copy.57, pred[7,64]{1,0:T(8,128)(4,1)S(1)} %get-tuple-element.30), kind=kLoop, calls=%fused_computation.4 | loop fusion | flops 1835008 | bytes 14680512 | tf_op jit(solution)/shard_map/jit(_take)/select_n | solution.py:35
  83.4 14.8 %copy.39 = f32[64,7,64,64]{3,0,1,2:T(8,128)} copy(f32[64,7,64,64]{2,1,3,0:T(8,128)} %select_bitcast_fusion) | data formatting | bytes 14680064 | tf_op jit(solution)/shard_map/jit(_take)/select_n | solution.py:35
  98.2 32.2 %constant_dynamic-update-slice_fusion.1 = (f32[64,96,64]{2,0,1:T(8,128)S(1)}, f32[64,64,64]{2,0,1:T(8,128)}) fusion(f32[64,7,64,64]{3,0,1,2:T(8,128)} %copy.39, f32[7,64,64,64]{3,2,1,0:T(8,128)} %reshape.85), kind=kOutput, calls=%fused_computation.75 | convolution fusion | flops 1409286144 | bytes 17825792 | tf_op jit(solution)/shard_map/zkec,kcer->zer/dot_general | solution.py:36
  130.5 3.2 gather_fusion.2
  133.6 2.9 fusion.25
  143.4 4.1 copy.41
  152.4 2.9 reshape.86
  158.6 6.4 %gather_fusion.3 = f32[448,64,64]{2,1,0:T(8,128)} fusion(f32[64,96,64]{2,0,1:T(8,128)S(1)} %copy_dynamic-update-slice_fusion, s32[1024]{0:T(1024)S(1)} %pad_clamp_fusion), kind=kCustom, calls=%fused_computation.3.clone | custom fusion | bytes 14681856 | tf_op jit(solution)/shard_map/jit(_take)/gather | solution.py:35
  165.1 32.1 %fusion.17 = f32[64,64,64]{2,0,1:T(8,128)S(1)} fusion(f32[7,64,64,64]{3,2,1,0:T(8,128)} %reshape.85, f32[7,64,64,64]{3,2,1,0:T(8,128)} %bitcast.81, pred[7,64]{0,1:T(8,128)(4,1)S(1)} %copy.42), kind=kOutput, calls=%fused_computation.25 | convolution fusion | flops 1411121152 | bytes 15729088 | tf_op jit(solution)/shard_map/zkec,kcer->zer/dot_general | solution.py:36
  200.0 5.6 %fusion.7 = f32[192,192]{0,1:T(8,128)} fusion(f32[64,4096]{1,0:T(8,128)} %reshape.92, f32[64,4096]{1,0:T(8,128)} %reshape.86, f32[64,4096]{1,0:T(8,128)S(1)} %copy-done), kind=kOutput, calls=%fused_computation.14 | convolution fusion | flops 1813512192 | bytes 3293184 | tf_op jit(solution)/shard_map/dot_general | solution.py:42
  206.3 246.1 %all-reduce.5.cloned.1.call-done = f32[192,192]{0,1:T(8,128)} async-done(((f32[192,192]{0,1:T(8,128)}), f32[192,192]{0,1:T(8,128)}) %all-reduce.5.cloned.1.call-update) | async-done | bytes 147472 | tf_op jit(solution)/shard_map/psum | solution.py:42
  454.4 11.7 %cholesky.51 = f32[128,128]{1,0:T(8,128)S(1)} custom-call(f32[128,128]{1,0:T(8,128)S(1)} %cholesky.124), custom_call_target="Cholesky" | custom-call | tf_op jit(solution)/shard_map/jit(cholesky)/cholesky | solution.py:43
  468.3 11.3 %custom-call.15 = f32[1,128,128]{1,2,0:T(8,128)} custom-call(f32[1,128,128]{2,1,0:T(8,128)} %get-tuple-element.45), custom_call_target="InvertDiagBlocksLowerTriangular" | custom-call | tf_op jit(solution)/shard_map/jit(cholesky)/cholesky | solution.py:43
  481.4 6.8 %cholesky.110 = f32[64,64]{1,0:T(8,128)S(1)} custom-call(f32[64,64]{1,0:T(8,128)} %convolution_subtract_fusion.1), custom_call_target="Cholesky" | custom-call | tf_op jit(solution)/shard_map/jit(cholesky)/cholesky | solution.py:43
  492.5 20.3 %custom-call.16 = f32[2,128,128]{1,2,0:T(8,128)} custom-call(f32[2,128,128]{2,1,0:T(8,128)S(1)} %pad_maximum_fusion), custom_call_target="InvertDiagBlocksLowerTriangular" | custom-call | tf_op jit(solution)/shard_map/jit(_solve_triangular)/triangular_solve | solution.py:44
  512.8 2.8 fusion.13
  (86 shorter events, 47.2 us)
Async XLA Ops:
  7.2 445.2 %all-reduce.5.cloned.1.call-start = ((), (), s32[]{:S(2)}) async-start(), calls=%async_computation | async-start | bytes 393216 | tf_op jit(solution)/shard_map/psum | solution.py:42
  8.6 10.5 %copy-start.6 = (pred[4,8]{1,0:T(4,128)(4,1)}, pred[4,8]{1,0:T(4,128)(4,1)S(1)}, u32[]{:S(2)}) copy-start(pred[4,8]{1,0:T(4,128)(4,1)S(1)} %compare_and_fusion.1) | copy-start | bytes 100
  15.9 18.5 %copy-start.8 = (s32[6,64]{1,0:T(8,128)S(1)}, s32[6,64]{1,0:T(8,128)}, u32[]{:S(2)}) copy-start(s32[6,64]{1,0:T(8,128)} %param.10) | copy-start | bytes 4612
  26.1 21.0 %collective-permute-start = (f32[64,512]{1,0:T(8,128)S(1)}, f32[64,512]{1,0:T(8,128)}, u32[]{:S(2)}, u32[]{:S(2)}) collective-permute-start(f32[64,512]{1,0:T(8,128)S(1)} %get-tuple-element.41), channel_id=1, source_target_pairs={{0,8},{8,16},{16,24},{24,32},{32,40},{40,48},{48,56},{56,64},{64,7... | collective-permute-start | bytes 393224 | tf_op jit(solution)/shard_map/ppermute | solution.py:10
  28.8 19.4 %collective-permute-start.1 = (f32[64,512]{1,0:T(8,128)}, f32[64,512]{1,0:T(8,128)}, u32[]{:S(2)}, u32[]{:S(2)}) collective-permute-start(f32[64,512]{1,0:T(8,128)} %get-tuple-element.40), channel_id=1, source_target_pairs={{0,248},{8,0},{16,8},{24,16},{32,24},{40,32},{48,40},{56,48},{64,5... | collective-permute-start | bytes 393224 | tf_op jit(solution)/shard_map/ppermute | solution.py:10
  29.3 19.9 %collective-permute-start.2 = (f32[64,512]{1,0:T(8,128)}, f32[64,512]{1,0:T(8,128)}, u32[]{:S(2)}, u32[]{:S(2)}) collective-permute-start(f32[64,512]{1,0:T(8,128)} %get-tuple-element.39), channel_id=1, source_target_pairs={{0,1},{1,2},{2,3},{3,4},{4,5},{5,6},{6,7},{7,0},{8,9},{9,10},{10,1... | collective-permute-start | bytes 393224 | tf_op jit(solution)/shard_map/ppermute | solution.py:10
  30.4 19.9 %collective-permute-start.3 = (f32[64,512]{1,0:T(8,128)}, f32[64,512]{1,0:T(8,128)S(1)}, u32[]{:S(2)}, u32[]{:S(2)}) collective-permute-start(f32[64,512]{1,0:T(8,128)} %get-tuple-element.38), channel_id=1, source_target_pairs={{0,7},{1,0},{2,1},{3,2},{4,3},{5,4},{6,5},{7,6},{8,15},{9,8},{10,9... | collective-permute-start | bytes 393224 | tf_op jit(solution)/shard_map/ppermute | solution.py:10
  98.2 35.4 %copy-start.7 = (pred[4,8]{1,0:T(4,128)(4,1)S(1)}, pred[4,8]{1,0:T(4,128)(4,1)}, u32[]{:S(2)}) copy-start(pred[4,8]{1,0:T(4,128)(4,1)} %copy-done.6) | copy-start | bytes 100
  140.7 14.6 %collective-permute-start.4 = (f32[64,512]{1,0:T(8,128)S(1)}, f32[64,512]{1,0:T(8,128)}, u32[]{:S(2)}, u32[]{:S(2)}) collective-permute-start(f32[64,512]{1,0:T(8,128)S(1)} %get-tuple-element.37), channel_id=1, source_target_pairs={{0,8},{8,16},{16,24},{24,32},{32,40},{40,48},{48,56},{56,64},{64,7... | collective-permute-start | bytes 393224 | tf_op jit(solution)/shard_map/ppermute | solution.py:10
  147.5 8.8 %collective-permute-start.5 = (f32[64,512]{1,0:T(8,128)}, f32[64,512]{1,0:T(8,128)}, u32[]{:S(2)}, u32[]{:S(2)}) collective-permute-start(f32[64,512]{1,0:T(8,128)} %get-tuple-element.36), channel_id=1, source_target_pairs={{0,248},{8,0},{16,8},{24,16},{32,24},{40,32},{48,40},{56,48},{64,5... | collective-permute-start | bytes 393224 | tf_op jit(solution)/shard_map/ppermute | solution.py:10
  149.7 7.7 %collective-permute-start.6 = (f32[64,512]{1,0:T(8,128)}, f32[64,512]{1,0:T(8,128)}, u32[]{:S(2)}, u32[]{:S(2)}) collective-permute-start(f32[64,512]{1,0:T(8,128)} %get-tuple-element.35), channel_id=1, source_target_pairs={{0,1},{1,2},{2,3},{3,4},{4,5},{5,6},{6,7},{7,0},{8,9},{9,10},{10,1... | collective-permute-start | bytes 393224 | tf_op jit(solution)/shard_map/ppermute | solution.py:10
  149.7 8.8 %collective-permute-start.7 = (f32[64,512]{1,0:T(8,128)}, f32[64,512]{1,0:T(8,128)S(1)}, u32[]{:S(2)}, u32[]{:S(2)}) collective-permute-start(f32[64,512]{1,0:T(8,128)} %get-tuple-element.34), channel_id=1, source_target_pairs={{0,7},{1,0},{2,1},{3,2},{4,3},{5,4},{6,5},{7,6},{8,15},{9,8},{10,9... | collective-permute-start | bytes 393224 | tf_op jit(solution)/shard_map/ppermute | solution.py:10
  197.1 2.9 copy-start
  200.0 5.7 %copy-start.5 = (pred[64,64]{1,0:T(8,128)(4,1)S(1)}, pred[64,64]{1,0:T(8,128)(4,1)}, u32[]{:S(2)}) copy-start(pred[64,64]{1,0:T(8,128)(4,1)} %iota_compare_fusion.4) | copy-start | bytes 12292
  200.0 312.8 %copy-start.1 = (f32[64,4096]{1,0:T(8,128)S(1)}, f32[64,4096]{1,0:T(8,128)}, u32[]{:S(2)}) copy-start(f32[64,4096]{1,0:T(8,128)} %reshape.86) | copy-start | bytes 3145732
  454.4 61.2 %copy-start.2 = (f32[64,4096]{1,0:T(8,128)S(1)}, f32[64,4096]{1,0:T(8,128)}, u32[]{:S(2)}) copy-start(f32[64,4096]{1,0:T(8,128)} %reshape.92) | copy-start | bytes 3145732
  466.1 0.6 copy-start.4
  490.9 0.7 copy-start.3
Sparse Core Ops, SparseCore 0:
  205.8 246.5 all-reduce.4
where the time goes:
time: 538 us; the launch traced here: 529 us
  waiting for transfers between devices  246 us (46%)
  local copies, waits for them, and re-layouts  97.8 us (18%)
  matrix products  78.3 us (15%)
  other arithmetic  75.9 us (14%)
  between operations  16 us (3%)
  starting transfers between devices  15.1 us (3%)
    psum x1, waiting for transfers between devices, shards(): lax.psum(jnp.dot(basis, basis.T, precision=lax.Precision.HIGHEST), ('sx',...  246 us
    dot_general x2, matrix products, apply_operator(): jnp.einsum('zkec,kcer->zer', picked, tiles, precision=lax.Precision.HIGHEST)  64.3 us
    another operation x7, other arithmetic, shards(): lower = jnp.linalg.cholesky(gram)  31.8 us
    gather x3, local copies, waits for them, and re-layouts, apply_operator(): picked = jnp.take(extended, index, axis=1)  27.7 us
    another operation x5, other arithmetic, shards(): orthonormal = jax.scipy.linalg.solve_triangular(lower, basis, lower=True)  22.5 us
    ppermute x8, starting transfers between devices, from_behind(): return lax.ppermute(value, axis, pairs)  15.1 us
    select_n x1, local copies, waits for them, and re-layouts, apply_operator(): picked = jnp.take(extended, index, axis=1)  14.8 us
    reshape x1, local copies, waits for them, and re-layouts, shards(): tiles = blocks.reshape(7, nodes, elems, nodes)  12.6 us
  transfers between devices with their start and end apart: 9, of which 1 were waited for; matrix products, arithmetic and copies ran while one was open for 5% of the time, Pallas kernels for 0%

commit v1 on v0

v1 whole, which is shorter than its diff:
```python
import functools
import math

import jax
import jax.numpy as jnp
from jax import lax
from jax.experimental import pallas as pl
from jax.experimental.pallas import tpu as pltpu
from jax.sharding import PartitionSpec as P

MESH = pl.DeviceIdType.MESH
F32 = jnp.float32
BF16 = jnp.bfloat16
HIGHEST = lax.Precision.HIGHEST


def split(value):
    high = value.astype(BF16)
    low = (value - high.astype(F32)).astype(BF16)
    return high, low


def exact_dot(a, b, contract):
    return lax.dot_general(a, b, ((contract[0:1], contract[1:2]), ((), ())), precision=HIGHEST, preferred_element_type=F32)


def factor(matrix):
    size = matrix.shape[0]
    rows = lax.broadcasted_iota(jnp.int32, (size, size), 0)
    cols = lax.broadcasted_iota(jnp.int32, (size, size), 1)
    wide = jnp.concatenate([matrix, jnp.where(rows == cols, 1.0, 0.0).astype(F32)], axis=1)
    parts = [wide[8 * b:8 * b + 8] for b in range(size // 8)]
    sub = lax.broadcasted_iota(jnp.int32, (8, 2 * size), 0)
    lane = lax.broadcasted_iota(jnp.int32, (8, 2 * size), 1)
    for j in range(size):
        home, at = j // 8, j % 8
        pivot_row = jnp.broadcast_to(parts[home][at:at + 1], (8, 2 * size))
        pivot = jnp.broadcast_to(parts[home][at:at + 1, j:j + 1], (8, 2 * size))
        scaled = pivot_row / pivot
        for b in range(home, size // 8):
            column = jnp.broadcast_to(parts[b][:, j:j + 1], (8, 2 * size))
            if b == home:
                column = jnp.where(sub > at, column, 0.0)
            parts[b] = parts[b] - column * scaled
    done = []
    for b in range(size // 8):
        diagonal = jnp.sum(jnp.where(lane == sub + 8 * b, parts[b], 0.0), axis=1, keepdims=True)
        scaled = parts[b] / jnp.sqrt(diagonal)
        done.append(jnp.where((lane < sub + 8 * b), 0.0, scaled))
    result = jnp.concatenate(done, axis=0)
    return result[:, :size], result[:, size:]


def basis_kernel(n_sx, n_sy, start_hbm, blocks_hbm, near_ref, lists_ref, high_hbm, low_hbm, upper_ref, inverse_ref,
                 start_vm, stage, tiles, ext_a, ext_b, high, low, send, recv, gram, chunks, mine, planes, whole,
                 start_sem, block_sem, out_sem, send_sem, recv_sem, sum_send, sum_recv):
    sx, sy = lax.axis_index("sx"), lax.axis_index("sy")
    count_rhs, rows = start_hbm.shape
    pairs = rows // 128
    groups = block_sem.shape[0]
    width = rows // groups
    per_group = width // 128

    start_copy = pltpu.make_async_copy(start_hbm, start_vm, start_sem)
    start_copy.start()
    block_copies = []
    for c in range(groups):
        copy = pltpu.make_async_copy(blocks_hbm.at[:, :, pl.ds(c * width, width)], stage.at[:, :, pl.ds(c * width, width)], block_sem.at[c])
        copy.start()
        block_copies.append(copy)

    barrier = pltpu.get_barrier_semaphore()

    @pl.loop(1, n_sx)
    def _(d):
        pl.semaphore_signal(barrier, inc=1, device_id=(lax.rem(sx + d, n_sx), sy), device_id_type=MESH)

    @pl.loop(1, n_sy)
    def _(d):
        pl.semaphore_signal(barrier, inc=1, device_id=(sx, lax.rem(sy + d, n_sy)), device_id_type=MESH)

    left_half = lax.broadcasted_iota(jnp.int32, (count_rhs, 128), 1) < 64

    def spread(pair, ext, slot):
        turned = pltpu.roll(pair, 64, 1)
        for side, both in enumerate((jnp.where(left_half, pair, turned), jnp.where(left_half, turned, pair))):
            h, l = split(both)
            ext[slot + side, 0] = h
            ext[slot + side, 1] = l

    def keep(pair, p, power):
        h, l = split(pair)
        at = pl.ds(pl.multiple_of(p * 128, 128), 128)
        high[power * count_rhs:(power + 1) * count_rhs, at] = h
        low[power * count_rhs:(power + 1) * count_rhs, at] = l

    def exchange(ext, turn):
        targets = (
            (lax.rem(sx + 1, n_sx), sy),
            (lax.rem(sx + n_sx - 1, n_sx), sy),
            (sx, lax.rem(sy + 1, n_sy)),
            (sx, lax.rem(sy + n_sy - 1, n_sy)),
        )
        copies = []
        for d in (2, 3, 0, 1):
            for g in range(4):
                first, second = lists_ref[0, 0, d, 2 * g], lists_ref[0, 0, d, 2 * g + 1]
                one = ext[first, 0].astype(F32) + ext[first, 1].astype(F32)
                two = ext[second, 0].astype(F32) + ext[second, 1].astype(F32)
                send[turn, d, g] = jnp.where(left_half, one, two)
            if turn == 0 and d == 2:
                pl.semaphore_wait(barrier, n_sx + n_sy - 2)
            copy = pltpu.make_async_remote_copy(
                src_ref=send.at[turn, d], dst_ref=recv.at[turn, d],
                send_sem=send_sem.at[turn, d], recv_sem=recv_sem.at[turn, d],
                device_id=targets[d], device_id_type=MESH)
            copy.start()
            copies.append((d, copy))
        return copies

    def arrive(copies, ext, turn):
        for d, copy in copies:
            copy.wait()
            for g in range(4):
                spread(recv[turn, d, g], ext, 64 + d * 8 + 2 * g)

    def power(ext, use):
        @pl.loop(0, pairs)
        def _(p):
            lhs = []
            for hl in range(2):
                for side in range(2):
                    e = 2 * p + side
                    slots = [e] + [near_ref[k, e] for k in range(6)] + [near_ref[5, e]]
                    lhs.append(jnp.concatenate(
                        [jnp.where(left_half, ext[slots[2 * k], hl], ext[slots[2 * k + 1], hl]) for k in range(4)], axis=1))
            out = jnp.dot(jnp.concatenate(lhs, axis=0), tiles[p], preferred_element_type=F32)
            out = out[:, :128] + out[:, 128:]
            out = out[:2 * count_rhs] + out[2 * count_rhs:]
            use(p, jnp.where(left_half, out[:count_rhs], out[count_rhs:]))

    start_copy.wait()

    @pl.loop(0, pairs)
    def _(p):
        pair = start_vm[:, pl.ds(pl.multiple_of(p * 128, 128), 128)]
        keep(pair, p, 0)
        spread(pair, ext_a, 2 * p)

    copies = exchange(ext_a, 0)

    for c in range(groups):
        block_copies[c].wait()

        @pl.loop(c * per_group, (c + 1) * per_group)
        def _(p):
            at = pl.ds(pl.multiple_of(p * 128, 128), 128)
            for k in range(7):
                h, l = split(stage[k, :, at])
                tiles[p, k * 64:(k + 1) * 64, 0:128] = h
                tiles[p, k * 64:(k + 1) * 64, 128:256] = l
            tiles[p, 448:512, :] = jnp.zeros((64, 256), BF16)

    arrive(copies, ext_a, 0)

    def first(p, pair):
        keep(pair, p, 1)
        spread(pair, ext_b, 2 * p)

    power(ext_a, first)
    copies = exchange(ext_b, 1)
    arrive(copies, ext_b, 1)
    power(ext_b, lambda p, pair: keep(pair, p, 2))

    out_copies = [pltpu.make_async_copy(high, high_hbm, out_sem.at[0]), pltpu.make_async_copy(low, low_hbm, out_sem.at[1])]
    for copy in out_copies:
        copy.start()

    size = 3 * count_rhs
    depth = 1024

    def inner(c, totals):
        at = pl.ds(pl.multiple_of(c * depth, depth), depth)
        h, l = high[:, at], low[:, at]
        dims = (((1,), (1,)), ((), ()))
        return (totals[0] + lax.dot_general(h, h, dims, preferred_element_type=F32),
                totals[1] + lax.dot_general(h, l, dims, preferred_element_type=F32))

    zero = jnp.zeros((size, size), F32)
    straight, crossed = lax.fori_loop(0, rows // depth, inner, (zero, zero))
    local = straight + crossed + crossed.T
    per = gram.shape[1]
    gram[0:size // per] = local[:, :128].reshape(size // per, per, 128)
    corner = jnp.concatenate([local[128:, 128:], jnp.zeros((count_rhs, 128 - count_rhs), F32)], axis=1)
    gram[size // per:] = corner.reshape(count_rhs // per, per, 128)

    @pl.loop(1, n_sx)
    def _(d):
        other = lax.rem(sx + d, n_sx)
        pltpu.make_async_remote_copy(
            src_ref=gram.at[other], dst_ref=chunks.at[d - 1], send_sem=sum_send.at[0], recv_sem=sum_recv.at[0],
            device_id=(other, sy), device_id_type=MESH).start()

    pltpu.make_async_copy(chunks, chunks, sum_recv.at[0]).wait()
    part = gram[sx]
    for d in range(n_sx - 1):
        part = part + chunks[d]
    mine[...] = part
    planes[sy] = part

    @pl.loop(1, n_sy)
    def _(d):
        pltpu.make_async_remote_copy(
            src_ref=mine, dst_ref=planes.at[sy], send_sem=sum_send.at[1], recv_sem=sum_recv.at[1],
            device_id=(sx, lax.rem(sy + d, n_sy)), device_id_type=MESH).start()

    pltpu.make_async_copy(planes.at[pl.ds(0, n_sy - 1)], planes.at[pl.ds(0, n_sy - 1)], sum_recv.at[1]).wait()
    pltpu.make_async_copy(planes.at[pl.ds(0, n_sy - 1)], planes.at[pl.ds(0, n_sy - 1)], sum_send.at[1]).wait()
    part = planes[0]
    for d in range(1, n_sy):
        part = part + planes[d]
    mine[...] = part
    whole[sx] = part

    @pl.loop(1, n_sx)
    def _(d):
        pltpu.make_async_remote_copy(
            src_ref=mine, dst_ref=whole.at[sx], send_sem=sum_send.at[2], recv_sem=sum_recv.at[2],
            device_id=(lax.rem(sx + d, n_sx), sy), device_id_type=MESH).start()

    pltpu.make_async_copy(whole.at[pl.ds(0, n_sx - 1)], whole.at[pl.ds(0, n_sx - 1)], sum_recv.at[2]).wait()
    full = whole[...].reshape(n_sx * per, 128)

    u00, x00 = factor(full[0:64, 0:64])
    u01 = exact_dot(x00, full[0:64, 64:128], (1, 0))
    u11, x11 = factor(full[64:128, 64:128] - exact_dot(u01, u01, (0, 0)))
    x10 = -exact_dot(x11, exact_dot(u01, x00, (0, 0)), (1, 0))
    none = jnp.zeros((64, 64), F32)
    x1 = jnp.concatenate([jnp.concatenate([x00, none], axis=1), jnp.concatenate([x10, x11], axis=1)], axis=0)
    u2 = exact_dot(x1, full[128:192], (1, 1))
    u22, x22 = factor(full[192:256, 0:64] - exact_dot(u2, u2, (0, 0)))
    x2 = -exact_dot(x22, exact_dot(u2, x1, (0, 0)), (1, 0))
    upper_ref[0:64, 0:128] = jnp.concatenate([u00, u01], axis=1)
    upper_ref[64:128, 0:128] = jnp.concatenate([none, u11], axis=1)
    upper_ref[128:192, 0:128] = jnp.zeros((64, 128), F32)
    upper_ref[0:128, 128:192] = u2
    upper_ref[128:192, 128:192] = u22
    inverse_ref[0:128, 0:128] = x1
    inverse_ref[128:192, 0:128] = x2
    inverse_ref[0:128, 128:192] = jnp.zeros((128, 64), F32)
    inverse_ref[128:192, 128:192] = x22

    for copy in out_copies:
        copy.wait()
    pltpu.make_async_copy(chunks, chunks, sum_send.at[0]).wait()
    pltpu.make_async_copy(chunks, chunks, sum_send.at[2]).wait()


def result_kernel(scale, high_ref, low_ref, upper_ref, inverse_ref, q_ref, r_ref):
    xh, xl = split(inverse_ref[...] * scale)
    both = jnp.concatenate([xh, xl], axis=0)
    size = xh.shape[0]
    out = jnp.dot(both, high_ref[...], preferred_element_type=F32)
    q_ref[...] = out[:size] + out[size:] + jnp.dot(xh, low_ref[...], preferred_element_type=F32)
    r_ref[...] = upper_ref[...] / scale


def shards(n_sx, n_sy, start_block, blocks, neighbors, ghost_lists):
    count_rhs, rows = start_block.shape
    size = 3 * count_rhs
    pairs = rows // 128
    per = 256 // n_sx
    groups = 8
    anywhere = pl.BlockSpec(memory_space=pl.ANY)
    scalars = pl.BlockSpec(memory_space=pltpu.SMEM)
    vmem = pl.BlockSpec(memory_space=pltpu.VMEM)
    high, low, upper, inverse = pl.pallas_call(
        functools.partial(basis_kernel, n_sx, n_sy),
        out_shape=(
            jax.ShapeDtypeStruct((size, rows), BF16),
            jax.ShapeDtypeStruct((size, rows), BF16),
            jax.ShapeDtypeStruct((size, size), F32),
            jax.ShapeDtypeStruct((size, size), F32),
        ),
        in_specs=[anywhere, anywhere, scalars, scalars],
        out_specs=(anywhere, anywhere, vmem, vmem),
        scratch_shapes=[
            pltpu.VMEM((count_rhs, rows), F32),
            pltpu.VMEM((7, 64, rows), F32),
            pltpu.VMEM((pairs, 512, 256), BF16),
            pltpu.VMEM((96, 2, count_rhs, 128), BF16),
            pltpu.VMEM((96, 2, count_rhs, 128), BF16),
            pltpu.VMEM((size, rows), BF16),
            pltpu.VMEM((size, rows), BF16),
            pltpu.VMEM((2, 4, 4, count_rhs, 128), F32),
            pltpu.VMEM((2, 4, 4, count_rhs, 128), F32),
            pltpu.VMEM((n_sx, per, 128), F32),
            pltpu.VMEM((n_sx - 1, per, 128), F32),
            pltpu.VMEM((per, 128), F32),
            pltpu.VMEM((n_sy, per, 128), F32),
            pltpu.VMEM((n_sx, per, 128), F32),
            pltpu.SemaphoreType.DMA,
            pltpu.SemaphoreType.DMA((groups,)),
            pltpu.SemaphoreType.DMA((2,)),
            pltpu.SemaphoreType.DMA((2, 4)),
            pltpu.SemaphoreType.DMA((2, 4)),
            pltpu.SemaphoreType.DMA((3,)),
            pltpu.SemaphoreType.DMA((3,)),
        ],
        compiler_params=pltpu.CompilerParams(
            collective_id=0, has_side_effects=True, vmem_limit_bytes=48 * 1024 * 1024),
        name="basis_and_factor",
    )(start_block, blocks, neighbors, ghost_lists)

    scale = math.sqrt(rows * n_sx * n_sy)
    tile = 1024
    return pl.pallas_call(
        functools.partial(result_kernel, scale),
        grid=(rows // tile,),
        out_shape=(jax.ShapeDtypeStruct((size, rows), F32), jax.ShapeDtypeStruct((size, size), F32)),
        in_specs=[
            pl.BlockSpec((size, tile), lambda i: (0, i)),
            pl.BlockSpec((size, tile), lambda i: (0, i)),
            pl.BlockSpec((size, size), lambda i: (0, 0)),
            pl.BlockSpec((size, size), lambda i: (0, 0)),
        ],
        out_specs=(pl.BlockSpec((size, tile), lambda i: (0, i)), pl.BlockSpec((size, size), lambda i: (0, 0))),
        compiler_params=pltpu.CompilerParams(vmem_limit_bytes=32 * 1024 * 1024),
        name="orthonormal_rows",
    )(high, low, upper, inverse)


def solution(mesh):
    return jax.shard_map(
        functools.partial(shards, mesh.shape["sx"], mesh.shape["sy"]),
        mesh=mesh,
        in_specs=(
            P(None, ("sx", "sy")),
            P(None, None, ("sx", "sy")),
            P(None, ("sx", "sy")),
            P("sx", "sy", None, None),
        ),
        out_specs=(P(None, ("sx", "sy")), P()),
        check_vma=False,
    )
```

time: 538 us -> 91.5 us (0.17); the launches traced: 529 us -> 91.3 us
  waiting for transfers between devices: 246 us -> 0 us
  local copies, waits for them, and re-layouts: 97.8 us -> 2.59 us
  Pallas kernels: 0 us -> 88.1 us
  matrix products: 78.3 us -> 0 us
  other arithmetic: 75.9 us -> 0 us
  between operations: 16 us -> 0.65 us
  starting transfers between devices: 15.1 us -> 0 us
    psum x1 -> x0, waiting for transfers between devices: 246 us -> none  [shards(): lax.psum(jnp.dot(basis, basis.T, precision=lax.Precision.HIGHEST), ('sx',...]
    pallas_call x0 -> x2, Pallas kernels: none -> 88.1 us  [the longest x1 84.7 us: shards(): pl.pallas_call(functools.partial(basis_kernel, n_sx, n_sy), out_shape=(ja...]
    dot_general x3 -> x0, matrix products: 69.9 us -> none  [the longest x2 64.3 us: apply_operator(): jnp.einsum('zkec,kcer->zer', picked, tiles, precision=lax.Precision.HIGHEST)]
    another operation x12 -> x0, other arithmetic: 54.3 us -> none  [the longest x7 31.8 us: shards(): lower = jnp.linalg.cholesky(gram)]
    reshape x15 -> x0, local copies, waits for them, and re-layouts: 35.2 us -> none  [the longest x1 12.6 us: shards(): tiles = blocks.reshape(7, nodes, elems, nodes)]
    gather x5 -> x0, local copies, waits for them, and re-layouts: 34.1 us -> none  [the longest x3 27.7 us: apply_operator(): picked = jnp.take(extended, index, axis=1)]
    select_n x4 -> x0, other arithmetic: 18.1 us -> none  [the longest x1 11.6 us: apply_operator(): picked = jnp.take(extended, index, axis=1)]
    ppermute x8 -> x0, starting transfers between devices: 15.1 us -> none  [from_behind(): return lax.ppermute(value, axis, pairs)]
  transfers between devices with their start and end apart: 9 -> 0, of which waited for: 1 -> 0; matrix products, arithmetic and copies ran while one was open for 5% -> 0% of each run, Pallas kernels for 0% -> 0%
where the time goes in v1:
time: 91.5 us; the launch traced here: 91.3 us
  Pallas kernels  88.1 us (96%)
  local copies, waits for them, and re-layouts  2.59 us (3%)
    pallas_call x1, Pallas kernels, shards(): pl.pallas_call(functools.partial(basis_kernel, n_sx, n_sy), out_shape=(ja...  84.7 us
    pallas_call x1, Pallas kernels, shards(): pl.pallas_call(functools.partial(result_kernel, scale), grid=(rows // til...  3.37 us
    unnamed x6, local copies, waits for them, and re-layouts  2.59 us

profile of v1, /device:TPU:1, one launch (start us, length us, event | category | flops | bytes accessed | tf_op | source)
XLA Modules:
  0.0 91.3 jit_solution(4386048354903577512)
XLA Ops:
  0.6 0.0 copy-start
  0.6 1.2 %copy-done = f32[64,4096]{1,0:T(8,128)S(1)} copy-done((f32[64,4096]{1,0:T(8,128)S(1)}, f32[64,4096]{1,0:T(8,128)}, u32[]{:S(2)}) %copy-start) | copy-done | bytes 1048600
  1.9 0.0 copy-start.1
  1.9 0.7 copy-done.1
  2.5 0.0 copy-start.2
  2.5 0.7 copy-done.2
  3.2 84.7 %basis_and_factor.1 = (bf16[192,4096]{1,0:T(8,128)(2,1)S(1)}, bf16[192,4096]{1,0:T(8,128)(2,1)S(1)}, f32[192,192]{1,0:T(8,128)S(1)}, f32[192,192]{1,0:T(8,128)S(1)}) custom-call(f32[64,4096]{1,0:T(8,128)S(1)} %copy-done, f32[7,64,4096]{2,1,0:T(8,128)} %blocks_hbm.1, s32[6,64]{1,0:T(8,128)S(1)} %copy-done.1, s32[1,1,4,8]{3,2,1,0:T(4,128)S(1)} %copy-done.2), custom_call_target="tpu_custom_call" | custom-call | tf_op jit(solution)/shard_map/basis_and_factor/pallas_call | solution.py:277
  88.0 3.4 %orthonormal_rows.1 = (f32[192,4096]{1,0:T(8,128)}, f32[192,192]{1,0:T(8,128)}) custom-call(bf16[192,4096]{1,0:T(8,128)(2,1)S(1)} %get-tuple-element.6.high_ref, bf16[192,4096]{1,0:T(8,128)(2,1)S(1)} %get-tuple-element.7.low_ref, f32[192,192]{1,0:T(8,128)S(1)} %get-tuple-element.8.upper_ref, f32[192,192]{1,0:T(8,128)S(1)} %get-tuple-element.9.inverse_ref), custom_call_target="tpu_custom_call" | custom-call | tf_op jit(solution)/shard_map/orthonormal_rows/pallas_call | solution.py:317
Async XLA Ops:
  0.6 1.2 %copy-start = (f32[64,4096]{1,0:T(8,128)S(1)}, f32[64,4096]{1,0:T(8,128)}, u32[]{:S(2)}) copy-start(f32[64,4096]{1,0:T(8,128)} %start_hbm.1) | copy-start | bytes 3145732
  1.9 0.7 copy-start.1
  2.5 0.7 copy-start.2

commit v2 on v1

v2 whole, which is shorter than its diff:
```python
import functools
import math

import jax
import jax.numpy as jnp
from jax import lax
from jax.experimental import pallas as pl
from jax.experimental.pallas import tpu as pltpu
from jax.sharding import PartitionSpec as P

MESH = pl.DeviceIdType.MESH
F32 = jnp.float32
BF16 = jnp.bfloat16
HIGHEST = lax.Precision.HIGHEST


def split(value):
    high = value.astype(BF16)
    low = (value - high.astype(F32)).astype(BF16)
    return high, low


def exact_dot(a, b, contract):
    return lax.dot_general(a, b, ((contract[0:1], contract[1:2]), ((), ())), precision=HIGHEST, preferred_element_type=F32)


def factor(matrix):
    size = matrix.shape[0]
    shape = (8, 2 * size)
    count = size // 8
    rows = lax.broadcasted_iota(jnp.int32, (size, size), 0)
    cols = lax.broadcasted_iota(jnp.int32, (size, size), 1)
    wide = jnp.concatenate([matrix, jnp.where(rows == cols, 1.0, 0.0).astype(F32)], axis=1)
    parts = [wide[8 * b:8 * b + 8] for b in range(count)]
    sub = lax.broadcasted_iota(jnp.int32, shape, 0)
    lane = lax.broadcasted_iota(jnp.int32, shape, 1)
    done = []
    for t in range(count):
        spread_cols = [[jnp.broadcast_to(parts[b][:, 8 * t + k:8 * t + k + 1], shape) for b in range(t, count)] for k in range(8)]
        spread_rows = [jnp.broadcast_to(parts[t][i:i + 1], shape) for i in range(8)]
        entry = [[jnp.broadcast_to(spread_cols[k][0][i:i + 1], shape) for k in range(i + 1)] for i in range(8)]
        inverse = []
        for j in range(8):
            inverse.append(1.0 / entry[j][j])
            ratio = [None] * 8
            for i in range(j + 1, 8):
                ratio[i] = entry[i][j] * inverse[j]
                for k in range(j + 1, i + 1):
                    entry[i][k] = entry[i][k] - ratio[i] * entry[k][j]
                spread_rows[i] = spread_rows[i] - ratio[i] * spread_rows[j]
                for b in range(1, count - t):
                    spread_cols[i][b] = spread_cols[i][b] - ratio[i] * spread_cols[j][b]
            scaled = spread_rows[j] * inverse[j]
            for b in range(1, count - t):
                parts[t + b] = parts[t + b] - spread_cols[j][b] * scaled
        own = spread_rows[0] / jnp.sqrt(entry[0][0])
        for i in range(1, 8):
            own = jnp.where(sub == i, spread_rows[i] / jnp.sqrt(entry[i][i]), own)
        done.append(jnp.where(lane < sub + 8 * t, 0.0, own))
    result = jnp.concatenate(done, axis=0)
    return result[:, :size], result[:, size:]


def add_up(parts):
    while len(parts) > 1:
        parts = [parts[i] + parts[i + 1] if i + 1 < len(parts) else parts[i] for i in range(0, len(parts), 2)]
    return parts[0]


class SumOverDevices:
    def __init__(self, shape, place, refs, send_sem, recv_sem):
        self.n_sx, self.n_sy = shape
        self.sx, self.sy = place
        self.local, self.chunks, self.planes, self.whole = refs
        self.send_sem, self.recv_sem = send_sem, recv_sem

    def send(self, round_, source, target, device):
        pltpu.make_async_remote_copy(
            src_ref=source, dst_ref=target, send_sem=self.send_sem.at[round_], recv_sem=self.recv_sem.at[round_],
            device_id=device, device_id_type=MESH).start()

    def spans(self):
        return (self.chunks, self.planes.at[pl.ds(0, self.n_sy - 1)], self.whole.at[pl.ds(0, self.n_sx - 1)])

    def arrived(self, round_):
        span = self.spans()[round_]
        pltpu.make_async_copy(span, span, self.recv_sem.at[round_]).wait()

    def scatter(self, value):
        self.local[...] = value.reshape(self.local.shape)

        @pl.loop(1, self.n_sx)
        def _(d):
            other = lax.rem(self.sx + d, self.n_sx)
            self.send(0, self.local.at[other], self.chunks.at[d - 1], (other, self.sy))

    def exchange(self):
        self.arrived(0)
        self.planes[self.sy] = add_up([self.local[self.sx]] + [self.chunks[d] for d in range(self.n_sx - 1)])

        @pl.loop(1, self.n_sy)
        def _(d):
            mine = self.planes.at[self.sy]
            self.send(1, mine, mine, (self.sx, lax.rem(self.sy + d, self.n_sy)))

    def gather(self):
        self.arrived(1)
        self.whole[self.sx] = add_up([self.planes[d] for d in range(self.n_sy)])

        @pl.loop(1, self.n_sx)
        def _(d):
            mine = self.whole.at[self.sx]
            self.send(2, mine, mine, (lax.rem(self.sx + d, self.n_sx), self.sy))

    def result(self):
        self.arrived(2)
        return self.whole[...].reshape(-1, 128)

    def finish(self):
        for round_, span in enumerate(self.spans()):
            pltpu.make_async_copy(span, span, self.send_sem.at[round_]).wait()


def basis_kernel(n_sx, n_sy, start_hbm, blocks_hbm, near_hbm, lists_hbm, high_hbm, low_hbm, upper_ref, inverse_ref,
                 near_ref, lists_ref, start_vm, stage, tiles, ext_a, ext_b, high, low, send, recv,
                 local_1, chunks_1, planes_1, whole_1, local_2, chunks_2, planes_2, whole_2,
                 index_sem, start_sem, block_sem, out_sem, send_sem, recv_sem, sum_send_1, sum_recv_1, sum_send_2, sum_recv_2):
    sx, sy = lax.axis_index("sx"), lax.axis_index("sy")
    count_rhs, rows = start_hbm.shape
    pairs = rows // 128
    groups = block_sem.shape[0]
    width = rows // groups
    per_group = width // 128
    sum_1 = SumOverDevices((n_sx, n_sy), (sx, sy), (local_1, chunks_1, planes_1, whole_1), sum_send_1, sum_recv_1)
    sum_2 = SumOverDevices((n_sx, n_sy), (sx, sy), (local_2, chunks_2, planes_2, whole_2), sum_send_2, sum_recv_2)

    near_copy = pltpu.make_async_copy(near_hbm, near_ref, index_sem.at[0])
    lists_copy = pltpu.make_async_copy(lists_hbm, lists_ref, index_sem.at[1])
    start_copy = pltpu.make_async_copy(start_hbm, start_vm, start_sem)
    start_copy.start()
    lists_copy.start()
    near_copy.start()
    block_copies = []
    for c in range(groups):
        copy = pltpu.make_async_copy(blocks_hbm.at[:, :, pl.ds(c * width, width)], stage.at[:, :, pl.ds(c * width, width)], block_sem.at[c])
        copy.start()
        block_copies.append(copy)

    barrier = pltpu.get_barrier_semaphore()

    @pl.loop(1, n_sx)
    def _(d):
        pl.semaphore_signal(barrier, inc=1, device_id=(lax.rem(sx + d, n_sx), sy), device_id_type=MESH)

    @pl.loop(1, n_sy)
    def _(d):
        pl.semaphore_signal(barrier, inc=1, device_id=(sx, lax.rem(sy + d, n_sy)), device_id_type=MESH)

    left_half = lax.broadcasted_iota(jnp.int32, (count_rhs, 128), 1) < 64

    def spread(pair, ext, slot):
        turned = pltpu.roll(pair, 64, 1)
        for side, both in enumerate((jnp.where(left_half, pair, turned), jnp.where(left_half, turned, pair))):
            h, l = split(both)
            ext[slot + side, 0] = h
            ext[slot + side, 1] = l

    def keep(pair, p, power):
        h, l = split(pair)
        at = pl.ds(pl.multiple_of(p * 128, 128), 128)
        high[power * count_rhs:(power + 1) * count_rhs, at] = h
        low[power * count_rhs:(power + 1) * count_rhs, at] = l

    def exchange(ext, turn):
        targets = (
            (lax.rem(sx + 1, n_sx), sy),
            (lax.rem(sx + n_sx - 1, n_sx), sy),
            (sx, lax.rem(sy + 1, n_sy)),
            (sx, lax.rem(sy + n_sy - 1, n_sy)),
        )
        copies = {}
        for d in (2, 3, 0, 1):
            for g in range(4):
                first, second = lists_ref[0, 0, d, 2 * g], lists_ref[0, 0, d, 2 * g + 1]
                one = ext[first, 0].astype(F32) + ext[first, 1].astype(F32)
                two = ext[second, 0].astype(F32) + ext[second, 1].astype(F32)
                send[turn, d, g] = jnp.where(left_half, one, two)
            if turn == 0 and d == 2:
                pl.semaphore_wait(barrier, n_sx + n_sy - 2)
            copy = pltpu.make_async_remote_copy(
                src_ref=send.at[turn, d], dst_ref=recv.at[turn, d],
                send_sem=send_sem.at[turn, d], recv_sem=recv_sem.at[turn, d],
                device_id=targets[d], device_id_type=MESH)
            copy.start()
            copies[d] = copy
        return copies

    def arrive(copies, ext, turn):
        for d in range(4):
            copies[d].wait()
            for g in range(4):
                spread(recv[turn, d, g], ext, 64 + d * 8 + 2 * g)

    def power(ext, use):
        @pl.loop(0, pairs, unroll=8)
        def _(p):
            lhs = []
            for hl in range(2):
                for side in range(2):
                    e = 2 * p + side
                    slots = [e] + [near_ref[k, e] for k in range(6)] + [near_ref[5, e]]
                    lhs.append(jnp.concatenate(
                        [jnp.where(left_half, ext[slots[2 * k], hl], ext[slots[2 * k + 1], hl]) for k in range(4)], axis=1))
            out = jnp.dot(jnp.concatenate(lhs, axis=0), tiles[p], preferred_element_type=F32)
            out = out[:, :128] + out[:, 128:]
            out = out[:2 * count_rhs] + out[2 * count_rhs:]
            use(p, jnp.where(left_half, out[:count_rhs], out[count_rhs:]))

    start_copy.wait()

    @pl.loop(0, pairs, unroll=4)
    def _(p):
        pair = start_vm[:, pl.ds(pl.multiple_of(p * 128, 128), 128)]
        keep(pair, p, 0)
        spread(pair, ext_a, 2 * p)

    lists_copy.wait()
    near_copy.wait()
    copies = exchange(ext_a, 0)

    for c in range(groups):
        block_copies[c].wait()

        @pl.loop(c * per_group, (c + 1) * per_group)
        def _(p):
            at = pl.ds(pl.multiple_of(p * 128, 128), 128)
            for k in range(7):
                h, l = split(stage[k, :, at])
                tiles[p, k * 64:(k + 1) * 64, 0:128] = h
                tiles[p, k * 64:(k + 1) * 64, 128:256] = l
            tiles[p, 448:512, :] = jnp.zeros((64, 256), BF16)

    arrive(copies, ext_a, 0)

    def first(p, pair):
        keep(pair, p, 1)
        spread(pair, ext_b, 2 * p)

    power(ext_a, first)
    copies = exchange(ext_b, 1)

    depth = 1024
    dims = (((1,), (1,)), ((), ()))

    def products_1(c, total):
        at = pl.ds(pl.multiple_of(c * depth, depth), depth)
        h, l = high[0:2 * count_rhs, at], low[0:2 * count_rhs, at]
        return total + lax.dot_general(h, jnp.concatenate([h, l], axis=0), dims, preferred_element_type=F32)

    total = lax.fori_loop(0, rows // depth, products_1, jnp.zeros((128, 256), F32))
    sum_1.scatter(total[:, :128] + total[:, 128:] + total[:, 128:].T)

    arrive(copies, ext_b, 1)
    sum_1.exchange()
    power(ext_b, lambda p, pair: keep(pair, p, 2))
    sum_1.gather()

    def products_2(c, totals):
        at = pl.ds(pl.multiple_of(c * depth, depth), depth)
        new = jnp.concatenate([high[128:192, at], low[128:192, at]], axis=0)
        old = jnp.concatenate([high[0:128, at], low[0:128, at]], axis=0)
        return (totals[0] + lax.dot_general(new, old, dims, preferred_element_type=F32),
                totals[1] + lax.dot_general(new, new, dims, preferred_element_type=F32))

    across, corner = lax.fori_loop(0, rows // depth, products_2, (jnp.zeros((128, 256), F32), jnp.zeros((128, 128), F32)))
    across = across[:64, :128] + across[:64, 128:] + across[64:, :128]
    corner = corner[:64, :64] + corner[:64, 64:] + corner[64:, :64]
    sum_2.scatter(jnp.concatenate([across, jnp.concatenate([corner, jnp.zeros((64, 64), F32)], axis=1)], axis=0))

    out_copies = [pltpu.make_async_copy(high, high_hbm, out_sem.at[0]), pltpu.make_async_copy(low, low_hbm, out_sem.at[1])]
    for copy in out_copies:
        copy.start()

    none = jnp.zeros((64, 64), F32)
    full = sum_1.result()
    u00, x00 = factor(full[0:64, 0:64])
    u01 = exact_dot(x00, full[0:64, 64:128], (1, 0))
    s11 = full[64:128, 64:128] - exact_dot(u01, u01, (0, 0))
    sum_2.exchange()
    u11, x11 = factor(s11)
    sum_2.gather()
    x10 = -exact_dot(x11, exact_dot(u01, x00, (0, 0)), (1, 0))
    x1 = jnp.concatenate([jnp.concatenate([x00, none], axis=1), jnp.concatenate([x10, x11], axis=1)], axis=0)
    upper_ref[0:64, 0:128] = jnp.concatenate([u00, u01], axis=1)
    upper_ref[64:128, 0:128] = jnp.concatenate([none, u11], axis=1)
    upper_ref[128:192, 0:128] = jnp.zeros((64, 128), F32)
    inverse_ref[0:128, 0:128] = x1
    inverse_ref[0:128, 128:192] = jnp.zeros((128, 64), F32)

    full = sum_2.result()
    u2 = exact_dot(x1, full[0:64], (1, 1))
    u22, x22 = factor(full[64:128, 0:64] - exact_dot(u2, u2, (0, 0)))
    inverse_ref[128:192, 0:128] = -exact_dot(x22, exact_dot(u2, x1, (0, 0)), (1, 0))
    inverse_ref[128:192, 128:192] = x22
    upper_ref[0:128, 128:192] = u2
    upper_ref[128:192, 128:192] = u22

    for copy in out_copies:
        copy.wait()
    sum_1.finish()
    sum_2.finish()


def result_kernel(scale, high_ref, low_ref, upper_ref, inverse_ref, q_ref, r_ref):
    xh, xl = split(inverse_ref[...] * scale)
    both = jnp.concatenate([xh, xl], axis=0)
    size = xh.shape[0]
    out = jnp.dot(both, high_ref[...], preferred_element_type=F32)
    q_ref[...] = out[:size] + out[size:] + jnp.dot(xh, low_ref[...], preferred_element_type=F32)
    r_ref[...] = upper_ref[...] / scale


def shards(n_sx, n_sy, start_block, blocks, neighbors, ghost_lists):
    count_rhs, rows = start_block.shape
    size = 3 * count_rhs
    pairs = rows // 128
    per = 128 // n_sx
    groups = 8
    sum_buffers = [pltpu.VMEM((count, per, 128), F32) for count in (n_sx, n_sx - 1, n_sy, n_sx)]
    anywhere = pl.BlockSpec(memory_space=pl.ANY)
    in_hbm = pl.BlockSpec(memory_space=pltpu.HBM)
    vmem = pl.BlockSpec(memory_space=pltpu.VMEM)
    high, low, upper, inverse = pl.pallas_call(
        functools.partial(basis_kernel, n_sx, n_sy),
        out_shape=(
            jax.ShapeDtypeStruct((size, rows), BF16),
            jax.ShapeDtypeStruct((size, rows), BF16),
            jax.ShapeDtypeStruct((size, size), F32),
            jax.ShapeDtypeStruct((size, size), F32),
        ),
        in_specs=[in_hbm, in_hbm, in_hbm, in_hbm],
        out_specs=(anywhere, anywhere, vmem, vmem),
        scratch_shapes=[
            pltpu.SMEM(neighbors.shape, jnp.int32),
            pltpu.SMEM(ghost_lists.shape, jnp.int32),
            pltpu.VMEM((count_rhs, rows), F32),
            pltpu.VMEM((7, 64, rows), F32),
            pltpu.VMEM((pairs, 512, 256), BF16),
            pltpu.VMEM((96, 2, count_rhs, 128), BF16),
            pltpu.VMEM((96, 2, count_rhs, 128), BF16),
            pltpu.VMEM((size, rows), BF16),
            pltpu.VMEM((size, rows), BF16),
            pltpu.VMEM((2, 4, 4, count_rhs, 128), F32),
            pltpu.VMEM((2, 4, 4, count_rhs, 128), F32),
            *sum_buffers,
            *sum_buffers,
            pltpu.SemaphoreType.DMA((2,)),
            pltpu.SemaphoreType.DMA,
            pltpu.SemaphoreType.DMA((groups,)),
            pltpu.SemaphoreType.DMA((2,)),
            pltpu.SemaphoreType.DMA((2, 4)),
            pltpu.SemaphoreType.DMA((2, 4)),
            *[pltpu.SemaphoreType.DMA((3,))] * 4,
        ],
        compiler_params=pltpu.CompilerParams(
            collective_id=0, has_side_effects=True, vmem_limit_bytes=56 * 1024 * 1024),
        name="basis_and_factor",
    )(start_block, blocks, neighbors, ghost_lists)

    scale = math.sqrt(rows * n_sx * n_sy)
    tile = 1024
    return pl.pallas_call(
        functools.partial(result_kernel, scale),
        grid=(rows // tile,),
        out_shape=(jax.ShapeDtypeStruct((size, rows), F32), jax.ShapeDtypeStruct((size, size), F32)),
        in_specs=[
            pl.BlockSpec((size, tile), lambda i: (0, i)),
            pl.BlockSpec((size, tile), lambda i: (0, i)),
            pl.BlockSpec((size, size), lambda i: (0, 0)),
            pl.BlockSpec((size, size), lambda i: (0, 0)),
        ],
        out_specs=(pl.BlockSpec((size, tile), lambda i: (0, i)), pl.BlockSpec((size, size), lambda i: (0, 0))),
        compiler_params=pltpu.CompilerParams(vmem_limit_bytes=56 * 1024 * 1024),
        name="orthonormal_rows",
    )(high, low, upper, inverse)


def solution(mesh):
    return jax.shard_map(
        functools.partial(shards, mesh.shape["sx"], mesh.shape["sy"]),
        mesh=mesh,
        in_specs=(
            P(None, ("sx", "sy")),
            P(None, None, ("sx", "sy")),
            P(None, ("sx", "sy")),
            P("sx", "sy", None, None),
        ),
        out_specs=(P(None, ("sx", "sy")), P()),
        check_vma=False,
    )
```

time: 91.5 us -> 58.1 us (0.63)
  Pallas kernels: 88.1 us -> 57.3 us
  local copies, waits for them, and re-layouts: 2.59 us -> 0 us
    pallas_call x1, Pallas kernels: 84.7 us -> 52.1 us  [shards(): pl.pallas_call(functools.partial(basis_kernel, n_sx, n_sy), out_shape=(ja...]
    unnamed x6 -> x0, local copies, waits for them, and re-layouts: 2.59 us -> none
    pallas_call x1, Pallas kernels: 3.37 us -> 5.11 us  [shards(): pl.pallas_call(functools.partial(result_kernel, scale), grid=(rows // til...]
where the time goes in v2:
time: 58.1 us; the launch traced here: 57.9 us
  Pallas kernels  57.3 us (99%)
  between operations  0.64 us (1%)
    pallas_call x1, Pallas kernels, shards(): pl.pallas_call(functools.partial(basis_kernel, n_sx, n_sy), out_shape=(ja...  52.1 us
    pallas_call x1, Pallas kernels, shards(): pl.pallas_call(functools.partial(result_kernel, scale), grid=(rows // til...  5.11 us

profile of v2, /device:TPU:1, one launch (start us, length us, event | category | flops | bytes accessed | tf_op | source)
XLA Modules:
  0.0 57.9 jit_solution(9937282140754841332)
XLA Ops:
  0.6 52.1 %basis_and_factor.1 = (bf16[192,4096]{1,0:T(8,128)(2,1)}, bf16[192,4096]{1,0:T(8,128)(2,1)}, f32[192,192]{1,0:T(8,128)}, f32[192,192]{1,0:T(8,128)}) custom-call(f32[64,4096]{1,0:T(8,128)} %start_hbm.1, f32[7,64,4096]{2,1,0:T(8,128)} %blocks_hbm.1, s32[6,64]{1,0:T(8,128)} %near_hbm.1, s32[1,1,4,8]{3,2,1,0:T(4,128)} %lists_hbm.1), custom_call_target="tpu_custom_call" | custom-call | tf_op jit(solution)/shard_map/basis_and_factor/pallas_call | solution.py:333
  52.8 5.1 %orthonormal_rows.1 = (f32[192,4096]{1,0:T(8,128)}, f32[192,192]{1,0:T(8,128)}) custom-call(bf16[192,4096]{1,0:T(8,128)(2,1)} %get-tuple-element.6.high_ref, bf16[192,4096]{1,0:T(8,128)(2,1)} %get-tuple-element.7.low_ref, f32[192,192]{1,0:T(8,128)} %get-tuple-element.8.upper_ref, f32[192,192]{1,0:T(8,128)} %get-tuple-element.9.inverse_ref), custom_call_target="tpu_custom_call" | custom-call | tf_op jit(solution)/shard_map/orthonormal_rows/pallas_call | solution.py:372

commit v3 on v2

--- a/solution.py
+++ b/solution.py
@@ -67,10 +67,26 @@
     return parts[0]
 
 
+def ring_hops(d, n):
+    return min(d, n - d)
+
+
+def others_along(sx, sy, n_sx, n_sy):
+    n_x = 4 if n_sx == 32 else 1
+    n_y = n_sx // (2 * n_x)
+    x, y, core = sx // (2 * n_y), (sx // 2) % n_y, sx % 2
+    steps = [(dx, dy, dc) for dx in range(n_x) for dy in range(n_y) for dc in range(2)][1:]
+    steps.sort(key=lambda step: -(2 * ring_hops(step[0], n_x) + 2 * ring_hops(step[1], n_y) + step[2]))
+    along_x = [((lax.rem(x + dx, n_x) * n_y + lax.rem(y + dy, n_y)) * 2 + lax.rem(core + dc, 2)) for dx, dy, dc in steps]
+    along_y = [lax.rem(sy + d, n_sy) for d in sorted(range(1, n_sy), key=lambda d: -ring_hops(d, n_sy))]
+    return along_x, along_y
+
+
 class SumOverDevices:
-    def __init__(self, shape, place, refs, send_sem, recv_sem):
+    def __init__(self, shape, place, others, refs, send_sem, recv_sem):
         self.n_sx, self.n_sy = shape
         self.sx, self.sy = place
+        self.others_x, self.others_y = others
         self.local, self.chunks, self.planes, self.whole = refs
         self.send_sem, self.recv_sem = send_sem, recv_sem
 
@@ -89,28 +105,24 @@
     def scatter(self, value):
         self.local[...] = value.reshape(self.local.shape)
 
-        @pl.loop(1, self.n_sx)
-        def _(d):
-            other = lax.rem(self.sx + d, self.n_sx)
-            self.send(0, self.local.at[other], self.chunks.at[d - 1], (other, self.sy))
+        for slot, other in enumerate(self.others_x):
+            self.send(0, self.local.at[other], self.chunks.at[slot], (other, self.sy))
 
     def exchange(self):
         self.arrived(0)
         self.planes[self.sy] = add_up([self.local[self.sx]] + [self.chunks[d] for d in range(self.n_sx - 1)])
 
-        @pl.loop(1, self.n_sy)
-        def _(d):
-            mine = self.planes.at[self.sy]
-            self.send(1, mine, mine, (self.sx, lax.rem(self.sy + d, self.n_sy)))
+        mine = self.planes.at[self.sy]
+        for other in self.others_y:
+            self.send(1, mine, mine, (self.sx, other))
 
     def gather(self):
         self.arrived(1)
         self.whole[self.sx] = add_up([self.planes[d] for d in range(self.n_sy)])
 
-        @pl.loop(1, self.n_sx)
-        def _(d):
-            mine = self.whole.at[self.sx]
-            self.send(2, mine, mine, (lax.rem(self.sx + d, self.n_sx), self.sy))
+        mine = self.whole.at[self.sx]
+        for other in self.others_x:
+            self.send(2, mine, mine, (other, self.sy))
 
     def result(self):
         self.arrived(2)
@@ -131,8 +143,9 @@
     groups = block_sem.shape[0]
     width = rows // groups
     per_group = width // 128
-    sum_1 = SumOverDevices((n_sx, n_sy), (sx, sy), (local_1, chunks_1, planes_1, whole_1), sum_send_1, sum_recv_1)
-    sum_2 = SumOverDevices((n_sx, n_sy), (sx, sy), (local_2, chunks_2, planes_2, whole_2), sum_send_2, sum_recv_2)
+    others = others_along(sx, sy, n_sx, n_sy)
+    sum_1 = SumOverDevices((n_sx, n_sy), (sx, sy), others, (local_1, chunks_1, planes_1, whole_1), sum_send_1, sum_recv_1)
+    sum_2 = SumOverDevices((n_sx, n_sy), (sx, sy), others, (local_2, chunks_2, planes_2, whole_2), sum_send_2, sum_recv_2)
 
     near_copy = pltpu.make_async_copy(near_hbm, near_ref, index_sem.at[0])
     lists_copy = pltpu.make_async_copy(lists_hbm, lists_ref, index_sem.at[1])
@@ -202,7 +215,7 @@
                 spread(recv[turn, d, g], ext, 64 + d * 8 + 2 * g)
 
     def power(ext, use):
-        @pl.loop(0, pairs, unroll=8)
+        @pl.loop(0, pairs, unroll=16)
         def _(p):
             lhs = []
             for hl in range(2):
@@ -263,7 +276,6 @@
     arrive(copies, ext_b, 1)
     sum_1.exchange()
     power(ext_b, lambda p, pair: keep(pair, p, 2))
-    sum_1.gather()
 
     def products_2(c, totals):
         at = pl.ds(pl.multiple_of(c * depth, depth), depth)
@@ -281,14 +293,15 @@
     for copy in out_copies:
         copy.start()
 
+    sum_1.gather()
+    sum_2.exchange()
     none = jnp.zeros((64, 64), F32)
     full = sum_1.result()
     u00, x00 = factor(full[0:64, 0:64])
     u01 = exact_dot(x00, full[0:64, 64:128], (1, 0))
     s11 = full[64:128, 64:128] - exact_dot(u01, u01, (0, 0))
-    sum_2.exchange()
+    sum_2.gather()
     u11, x11 = factor(s11)
-    sum_2.gather()
     x10 = -exact_dot(x11, exact_dot(u01, x00, (0, 0)), (1, 0))
     x1 = jnp.concatenate([jnp.concatenate([x00, none], axis=1), jnp.concatenate([x10, x11], axis=1)], axis=0)
     upper_ref[0:64, 0:128] = jnp.concatenate([u00, u01], axis=1)
@@ -311,13 +324,38 @@
     sum_2.finish()
 
 
-def result_kernel(scale, high_ref, low_ref, upper_ref, inverse_ref, q_ref, r_ref):
-    xh, xl = split(inverse_ref[...] * scale)
-    both = jnp.concatenate([xh, xl], axis=0)
-    size = xh.shape[0]
-    out = jnp.dot(both, high_ref[...], preferred_element_type=F32)
-    q_ref[...] = out[:size] + out[size:] + jnp.dot(xh, low_ref[...], preferred_element_type=F32)
-    r_ref[...] = upper_ref[...] / scale
+def result_kernel(scale, high_hbm, low_hbm, upper_hbm, inverse_hbm, q_hbm, r_hbm, high, low, q, upper, inverse, r, in_sem, out_sem, small_sem):
+    chunks = out_sem.shape[0]
+    width = q.shape[1] // chunks
+    loads, stores = [], []
+    for c in range(chunks):
+        at = pl.ds(c * width, width)
+        loads.append((pltpu.make_async_copy(high_hbm.at[:, at], high.at[:, at], in_sem.at[0, c]),
+                      pltpu.make_async_copy(low_hbm.at[:, at], low.at[:, at], in_sem.at[1, c])))
+        stores.append(pltpu.make_async_copy(q.at[:, at], q_hbm.at[:, at], out_sem.at[c]))
+    small = [pltpu.make_async_copy(inverse_hbm, inverse, small_sem.at[0]), pltpu.make_async_copy(upper_hbm, upper, small_sem.at[1])]
+    small[0].start()
+    for pair in loads:
+        for copy in pair:
+            copy.start()
+    small[1].start()
+    small[0].wait()
+    xh, xl = split(inverse[...] * scale)
+    left = jnp.concatenate([xh, xh, xl], axis=1)
+    for c in range(chunks):
+        for copy in loads[c]:
+            copy.wait()
+        at = pl.ds(c * width, width)
+        h = high[:, at]
+        q[:, at] = jnp.dot(left, jnp.concatenate([h, low[:, at], h], axis=0), preferred_element_type=F32)
+        stores[c].start()
+        if c == 0:
+            small[1].wait()
+            r[...] = upper[...] / scale
+            stores.append(pltpu.make_async_copy(r, r_hbm, small_sem.at[2]))
+            stores[-1].start()
+    for store in stores:
+        store.wait()
 
 
 def shards(n_sx, n_sy, start_block, blocks, neighbors, ghost_lists):
@@ -368,18 +406,23 @@
     )(start_block, blocks, neighbors, ghost_lists)
 
     scale = math.sqrt(rows * n_sx * n_sy)
-    tile = 1024
+    parts = 4
     return pl.pallas_call(
         functools.partial(result_kernel, scale),
-        grid=(rows // tile,),
         out_shape=(jax.ShapeDtypeStruct((size, rows), F32), jax.ShapeDtypeStruct((size, size), F32)),
-        in_specs=[
-            pl.BlockSpec((size, tile), lambda i: (0, i)),
-            pl.BlockSpec((size, tile), lambda i: (0, i)),
-            pl.BlockSpec((size, size), lambda i: (0, 0)),
-            pl.BlockSpec((size, size), lambda i: (0, 0)),
+        in_specs=[anywhere] * 4,
+        out_specs=(anywhere, anywhere),
+        scratch_shapes=[
+            pltpu.VMEM((size, rows), BF16),
+            pltpu.VMEM((size, rows), BF16),
+            pltpu.VMEM((size, rows), F32),
+            pltpu.VMEM((size, size), F32),
+            pltpu.VMEM((size, size), F32),
+            pltpu.VMEM((size, size), F32),
+            pltpu.SemaphoreType.DMA((2, parts)),
+            pltpu.SemaphoreType.DMA((parts,)),
+            pltpu.SemaphoreType.DMA((3,)),
         ],
-        out_specs=(pl.BlockSpec((size, tile), lambda i: (0, i)), pl.BlockSpec((size, size), lambda i: (0, 0))),
         compiler_params=pltpu.CompilerParams(vmem_limit_bytes=56 * 1024 * 1024),
         name="orthonormal_rows",
     )(high, low, upper, inverse)

time: 58.1 us -> 54.2 us (0.933)
  Pallas kernels: 57.3 us -> 53.5 us
    pallas_call x1, Pallas kernels: 52.1 us -> 48.8 us  [shards(): pl.pallas_call(functools.partial(basis_kernel, n_sx, n_sy), out_shape=(ja...]
where the time goes in v3:
time: 54.2 us; the launch traced here: 54.1 us
  Pallas kernels  53.5 us (99%)
  between operations  0.64 us (1%)
    pallas_call x1, Pallas kernels, shards(): pl.pallas_call(functools.partial(basis_kernel, n_sx, n_sy), out_shape=(ja...  48.8 us
    pallas_call x1, Pallas kernels, shards(): pl.pallas_call(functools.partial(result_kernel, scale), out_shape=(jax.Sh...  4.7 us

profile of v3, /device:TPU:1, one launch (start us, length us, event | category | flops | bytes accessed | tf_op | source)
XLA Modules:
  0.0 54.1 jit_solution(7476394971603015387)
XLA Ops:
  0.6 48.8 %basis_and_factor.1 = (bf16[192,4096]{1,0:T(8,128)(2,1)}, bf16[192,4096]{1,0:T(8,128)(2,1)}, f32[192,192]{1,0:T(8,128)}, f32[192,192]{1,0:T(8,128)}) custom-call(f32[64,4096]{1,0:T(8,128)} %start_hbm.1, f32[7,64,4096]{2,1,0:T(8,128)} %blocks_hbm.1, s32[6,64]{1,0:T(8,128)} %near_hbm.1, s32[1,1,4,8]{3,2,1,0:T(4,128)} %lists_hbm.1), custom_call_target="tpu_custom_call" | custom-call | tf_op jit(solution)/shard_map/basis_and_factor/pallas_call | solution.py:371
  49.4 4.7 %orthonormal_rows.1 = (f32[192,4096]{1,0:T(8,128)}, f32[192,192]{1,0:T(8,128)}) custom-call(bf16[192,4096]{1,0:T(8,128)(2,1)} %get-tuple-element.6.high_hbm, bf16[192,4096]{1,0:T(8,128)(2,1)} %get-tuple-element.7.low_hbm, f32[192,192]{1,0:T(8,128)} %get-tuple-element.8.upper_hbm, f32[192,192]{1,0:T(8,128)} %get-tuple-element.9.inverse_hbm), custom_call_target="tpu_custom_call" | custom-call | tf_op jit(solution)/shard_map/orthonormal_rows/pallas_call | solution.py:410

commit v4 on v3

--- a/solution.py
+++ b/solution.py
@@ -149,8 +149,14 @@
 
     near_copy = pltpu.make_async_copy(near_hbm, near_ref, index_sem.at[0])
     lists_copy = pltpu.make_async_copy(lists_hbm, lists_ref, index_sem.at[1])
-    start_copy = pltpu.make_async_copy(start_hbm, start_vm, start_sem)
-    start_copy.start()
+    start_groups = start_sem.shape[0]
+    start_width = rows // start_groups
+    start_copies = []
+    for c in range(start_groups):
+        at = pl.ds(c * start_width, start_width)
+        copy = pltpu.make_async_copy(start_hbm.at[:, at], start_vm.at[:, at], start_sem.at[c])
+        copy.start()
+        start_copies.append(copy)
     lists_copy.start()
     near_copy.start()
     block_copies = []
@@ -214,8 +220,8 @@
             for g in range(4):
                 spread(recv[turn, d, g], ext, 64 + d * 8 + 2 * g)
 
-    def power(ext, use):
-        @pl.loop(0, pairs, unroll=16)
+    def power(ext, use, first_pair, last_pair):
+        @pl.loop(first_pair, last_pair, unroll=16)
         def _(p):
             lhs = []
             for hl in range(2):
@@ -229,13 +235,14 @@
             out = out[:2 * count_rhs] + out[2 * count_rhs:]
             use(p, jnp.where(left_half, out[:count_rhs], out[count_rhs:]))
 
-    start_copy.wait()
-
-    @pl.loop(0, pairs, unroll=4)
-    def _(p):
-        pair = start_vm[:, pl.ds(pl.multiple_of(p * 128, 128), 128)]
-        keep(pair, p, 0)
-        spread(pair, ext_a, 2 * p)
+    for c in range(start_groups):
+        start_copies[c].wait()
+
+        @pl.loop(c * start_width // 128, (c + 1) * start_width // 128, unroll=4)
+        def _(p):
+            pair = start_vm[:, pl.ds(pl.multiple_of(p * 128, 128), 128)]
+            keep(pair, p, 0)
+            spread(pair, ext_a, 2 * p)
 
     lists_copy.wait()
     near_copy.wait()
@@ -259,7 +266,7 @@
         keep(pair, p, 1)
         spread(pair, ext_b, 2 * p)
 
-    power(ext_a, first)
+    power(ext_a, first, 0, pairs)
     copies = exchange(ext_b, 1)
 
     depth = 1024
@@ -274,8 +281,9 @@
     sum_1.scatter(total[:, :128] + total[:, 128:] + total[:, 128:].T)
 
     arrive(copies, ext_b, 1)
+    power(ext_b, lambda p, pair: keep(pair, p, 2), 0, pairs // 2)
     sum_1.exchange()
-    power(ext_b, lambda p, pair: keep(pair, p, 2))
+    power(ext_b, lambda p, pair: keep(pair, p, 2), pairs // 2, pairs)
 
     def products_2(c, totals):
         at = pl.ds(pl.multiple_of(c * depth, depth), depth)
@@ -324,12 +332,10 @@
     sum_2.finish()
 
 
-def result_kernel(scale, high_hbm, low_hbm, upper_hbm, inverse_hbm, q_hbm, r_hbm, high, low, q, upper, inverse, r, in_sem, out_sem, small_sem):
-    chunks = out_sem.shape[0]
-    width = q.shape[1] // chunks
+def result_kernel(scale, spans, high_hbm, low_hbm, upper_hbm, inverse_hbm, q_hbm, r_hbm, high, low, q, upper, inverse, r, in_sem, out_sem, small_sem):
     loads, stores = [], []
-    for c in range(chunks):
-        at = pl.ds(c * width, width)
+    for c, at in enumerate(spans):
+        at = pl.ds(*at)
         loads.append((pltpu.make_async_copy(high_hbm.at[:, at], high.at[:, at], in_sem.at[0, c]),
                       pltpu.make_async_copy(low_hbm.at[:, at], low.at[:, at], in_sem.at[1, c])))
         stores.append(pltpu.make_async_copy(q.at[:, at], q_hbm.at[:, at], out_sem.at[c]))
@@ -342,10 +348,10 @@
     small[0].wait()
     xh, xl = split(inverse[...] * scale)
     left = jnp.concatenate([xh, xh, xl], axis=1)
-    for c in range(chunks):
+    for c, at in enumerate(spans):
         for copy in loads[c]:
             copy.wait()
-        at = pl.ds(c * width, width)
+        at = pl.ds(*at)
         h = high[:, at]
         q[:, at] = jnp.dot(left, jnp.concatenate([h, low[:, at], h], axis=0), preferred_element_type=F32)
         stores[c].start()
@@ -393,7 +399,7 @@
             *sum_buffers,
             *sum_buffers,
             pltpu.SemaphoreType.DMA((2,)),
-            pltpu.SemaphoreType.DMA,
+            pltpu.SemaphoreType.DMA((4,)),
             pltpu.SemaphoreType.DMA((groups,)),
             pltpu.SemaphoreType.DMA((2,)),
             pltpu.SemaphoreType.DMA((2, 4)),
@@ -406,9 +412,11 @@
     )(start_block, blocks, neighbors, ghost_lists)
 
     scale = math.sqrt(rows * n_sx * n_sy)
-    parts = 4
+    cuts = [0, rows // 4, rows // 2, 3 * rows // 4, rows]
+    spans = [(low_end, high_end - low_end) for low_end, high_end in zip(cuts[:-1], cuts[1:])]
+    parts = len(spans)
     return pl.pallas_call(
-        functools.partial(result_kernel, scale),
+        functools.partial(result_kernel, scale, spans),
         out_shape=(jax.ShapeDtypeStruct((size, rows), F32), jax.ShapeDtypeStruct((size, size), F32)),
         in_specs=[anywhere] * 4,
         out_specs=(anywhere, anywhere),

time: 54.2 us -> 54.4 us (level)
  no operation moved by 1% of the time
where the time goes in v4:
time: 54.4 us
  Pallas kernels  53.6 us (99%)
  between operations  0.8 us (1%)
    pallas_call x1, Pallas kernels, shards(): pl.pallas_call(functools.partial(basis_kernel, n_sx, n_sy), out_shape=(ja...  48.9 us
    pallas_call x1, Pallas kernels, shards(): pl.pallas_call(functools.partial(result_kernel, scale, spans), out_shape=...  4.7 us

profile of v4, /device:TPU:1, one launch (start us, length us, event | category | flops | bytes accessed | tf_op | source)
XLA Modules:
  0.0 54.4 jit_solution(10707727467835998733)
XLA Ops:
  0.6 48.9 %basis_and_factor.1 = (bf16[192,4096]{1,0:T(8,128)(2,1)}, bf16[192,4096]{1,0:T(8,128)(2,1)}, f32[192,192]{1,0:T(8,128)}, f32[192,192]{1,0:T(8,128)}) custom-call(f32[64,4096]{1,0:T(8,128)} %start_hbm.1, f32[7,64,4096]{2,1,0:T(8,128)} %blocks_hbm.1, s32[6,64]{1,0:T(8,128)} %near_hbm.1, s32[1,1,4,8]{3,2,1,0:T(4,128)} %lists_hbm.1), custom_call_target="tpu_custom_call" | custom-call | tf_op jit(solution)/shard_map/basis_and_factor/pallas_call | solution.py:377
  49.5 4.7 %orthonormal_rows.1 = (f32[192,4096]{1,0:T(8,128)}, f32[192,192]{1,0:T(8,128)}) custom-call(bf16[192,4096]{1,0:T(8,128)(2,1)} %get-tuple-element.6.high_hbm, bf16[192,4096]{1,0:T(8,128)(2,1)} %get-tuple-element.7.low_hbm, f32[192,192]{1,0:T(8,128)} %get-tuple-element.8.upper_hbm, f32[192,192]{1,0:T(8,128)} %get-tuple-element.9.inverse_hbm), custom_call_target="tpu_custom_call" | custom-call | tf_op jit(solution)/shard_map/orthonormal_rows/pallas_call | solution.py:418

commit v5 on v4

--- a/solution.py
+++ b/solution.py
@@ -79,7 +79,14 @@
     steps.sort(key=lambda step: -(2 * ring_hops(step[0], n_x) + 2 * ring_hops(step[1], n_y) + step[2]))
     along_x = [((lax.rem(x + dx, n_x) * n_y + lax.rem(y + dy, n_y)) * 2 + lax.rem(core + dc, 2)) for dx, dy, dc in steps]
     along_y = [lax.rem(sy + d, n_sy) for d in sorted(range(1, n_sy), key=lambda d: -ring_hops(d, n_sy))]
-    return along_x, along_y
+    same_x = [other for other, step in zip(along_x, steps) if step[0] == 0]
+    same_yc = [other for other, step in zip(along_x, steps) if step[1] == step[2] == 0]
+    two_off = [lax.rem(sy + d, n_sy) for d in sorted({2 % n_sy, (n_sy - 2) % n_sy} - {0})]
+    one_off = [lax.rem(sy + d, n_sy) for d in sorted({1, n_sy - 1})]
+    beside = [lax.rem(sx + d, n_sx) for d in (1, n_sx - 1)]
+    greeted = [(other, sy) for other in beside + same_yc + same_x] + [(sx, other) for other in one_off + two_off]
+    told = [(other, sy) for other in same_x] + [(sx, other) for other in two_off]
+    return (along_x, along_y), greeted, told
 
 
 class SumOverDevices:
@@ -136,14 +143,14 @@
 def basis_kernel(n_sx, n_sy, start_hbm, blocks_hbm, near_hbm, lists_hbm, high_hbm, low_hbm, upper_ref, inverse_ref,
                  near_ref, lists_ref, start_vm, stage, tiles, ext_a, ext_b, high, low, send, recv,
                  local_1, chunks_1, planes_1, whole_1, local_2, chunks_2, planes_2, whole_2,
-                 index_sem, start_sem, block_sem, out_sem, send_sem, recv_sem, sum_send_1, sum_recv_1, sum_send_2, sum_recv_2):
+                 index_sem, start_sem, block_sem, out_sem, send_sem, recv_sem, sum_send_1, sum_recv_1, sum_send_2, sum_recv_2, told_sem):
     sx, sy = lax.axis_index("sx"), lax.axis_index("sy")
     count_rhs, rows = start_hbm.shape
     pairs = rows // 128
     groups = block_sem.shape[0]
     width = rows // groups
     per_group = width // 128
-    others = others_along(sx, sy, n_sx, n_sy)
+    others, greeted, told = others_along(sx, sy, n_sx, n_sy)
     sum_1 = SumOverDevices((n_sx, n_sy), (sx, sy), others, (local_1, chunks_1, planes_1, whole_1), sum_send_1, sum_recv_1)
     sum_2 = SumOverDevices((n_sx, n_sy), (sx, sy), others, (local_2, chunks_2, planes_2, whole_2), sum_send_2, sum_recv_2)
 
@@ -167,13 +174,8 @@
 
     barrier = pltpu.get_barrier_semaphore()
 
-    @pl.loop(1, n_sx)
-    def _(d):
-        pl.semaphore_signal(barrier, inc=1, device_id=(lax.rem(sx + d, n_sx), sy), device_id_type=MESH)
-
-    @pl.loop(1, n_sy)
-    def _(d):
-        pl.semaphore_signal(barrier, inc=1, device_id=(sx, lax.rem(sy + d, n_sy)), device_id_type=MESH)
+    for device in greeted:
+        pl.semaphore_signal(barrier, inc=1, device_id=device, device_id_type=MESH)
 
     left_half = lax.broadcasted_iota(jnp.int32, (count_rhs, 128), 1) < 64
 
@@ -205,7 +207,9 @@
                 two = ext[second, 0].astype(F32) + ext[second, 1].astype(F32)
                 send[turn, d, g] = jnp.where(left_half, one, two)
             if turn == 0 and d == 2:
-                pl.semaphore_wait(barrier, n_sx + n_sy - 2)
+                pl.semaphore_wait(barrier, len(greeted))
+                for device in told:
+                    pl.semaphore_signal(told_sem, inc=1, device_id=device, device_id_type=MESH)
             copy = pltpu.make_async_remote_copy(
                 src_ref=send.at[turn, d], dst_ref=recv.at[turn, d],
                 send_sem=send_sem.at[turn, d], recv_sem=recv_sem.at[turn, d],
@@ -278,6 +282,7 @@
         return total + lax.dot_general(h, jnp.concatenate([h, l], axis=0), dims, preferred_element_type=F32)
 
     total = lax.fori_loop(0, rows // depth, products_1, jnp.zeros((128, 256), F32))
+    pl.semaphore_wait(told_sem, len(told))
     sum_1.scatter(total[:, :128] + total[:, 128:] + total[:, 128:].T)
 
     arrive(copies, ext_b, 1)
@@ -347,13 +352,14 @@
     small[1].start()
     small[0].wait()
     xh, xl = split(inverse[...] * scale)
-    left = jnp.concatenate([xh, xh, xl], axis=1)
     for c, at in enumerate(spans):
         for copy in loads[c]:
             copy.wait()
         at = pl.ds(*at)
         h = high[:, at]
-        q[:, at] = jnp.dot(left, jnp.concatenate([h, low[:, at], h], axis=0), preferred_element_type=F32)
+        l = low[:, at]
+        q[:, at] = (jnp.dot(xh, h, preferred_element_type=F32) + jnp.dot(xh, l, preferred_element_type=F32)
+                    + jnp.dot(xl, h, preferred_element_type=F32))
         stores[c].start()
         if c == 0:
             small[1].wait()
@@ -405,6 +411,7 @@
             pltpu.SemaphoreType.DMA((2, 4)),
             pltpu.SemaphoreType.DMA((2, 4)),
             *[pltpu.SemaphoreType.DMA((3,))] * 4,
+            pltpu.SemaphoreType.REGULAR,
         ],
         compiler_params=pltpu.CompilerParams(
             collective_id=0, has_side_effects=True, vmem_limit_bytes=56 * 1024 * 1024),

time: 54.4 us -> 53.4 us (0.982)
  Pallas kernels: 53.6 us -> 52.5 us
    pallas_call x1, Pallas kernels: 48.9 us -> 47.9 us  [shards(): pl.pallas_call(functools.partial(basis_kernel, n_sx, n_sy), out_shape=(ja...]
where the time goes in v5:
time: 53.4 us; the launch traced here: 53.3 us
  Pallas kernels  52.5 us (98%)
  between operations  0.8 us (1%)
    pallas_call x1, Pallas kernels, shards(): pl.pallas_call(functools.partial(basis_kernel, n_sx, n_sy), out_shape=(ja...  47.9 us
    pallas_call x1, Pallas kernels, shards(): pl.pallas_call(functools.partial(result_kernel, scale, spans), out_shape=...  4.57 us

profile of v5, /device:TPU:1, one launch (start us, length us, event | category | flops | bytes accessed | tf_op | source)
XLA Modules:
  0.0 53.3 jit_solution(7680879622434875269)
XLA Ops:
  0.6 47.9 %basis_and_factor.1 = (bf16[192,4096]{1,0:T(8,128)(2,1)}, bf16[192,4096]{1,0:T(8,128)(2,1)}, f32[192,192]{1,0:T(8,128)}, f32[192,192]{1,0:T(8,128)}) custom-call(f32[64,4096]{1,0:T(8,128)} %start_hbm.1, f32[7,64,4096]{2,1,0:T(8,128)} %blocks_hbm.1, s32[6,64]{1,0:T(8,128)} %near_hbm.1, s32[1,1,4,8]{3,2,1,0:T(4,128)} %lists_hbm.1), custom_call_target="tpu_custom_call" | custom-call | tf_op jit(solution)/shard_map/basis_and_factor/pallas_call | solution.py:383
  48.6 4.6 %orthonormal_rows.1 = (f32[192,4096]{1,0:T(8,128)}, f32[192,192]{1,0:T(8,128)}) custom-call(bf16[192,4096]{1,0:T(8,128)(2,1)} %get-tuple-element.6.high_hbm, bf16[192,4096]{1,0:T(8,128)(2,1)} %get-tuple-element.7.low_hbm, f32[192,192]{1,0:T(8,128)} %get-tuple-element.8.upper_hbm, f32[192,192]{1,0:T(8,128)} %get-tuple-element.9.inverse_hbm), custom_call_target="tpu_custom_call" | custom-call | tf_op jit(solution)/shard_map/orthonormal_rows/pallas_call | solution.py:425
